TPU v7x, 32 devices: a whole 2x2x4 slice. The times are simulated.
32 devices in a mesh: dp: 2 (over y), section: 4 (over x, core), tensor: 4 (over z).
Axes of the slice: x: 2, y: 2, z: 4, core: 2. Of those that a mesh axis runs over, the one named last changes fastest.
Arguments:
- sent_cot: bfloat16 [2, 4, 2, 56, 8192], P('dp', 'section', None, 'tensor'), may hold values from -6 to 6
- saved_heads: bfloat16 [2, 4, 2, 56, 1024], P('dp', 'section', None, None, 'tensor'), may hold values from -0.29882812 to 0.29882812
- out_proj: bfloat16 [4, 8192, 1024], P('section', None, 'tensor'), may hold values from -0.0625 to 0.0625
Outputs:
- head_grads: bfloat16 [2, 4, 2, 56, 1024], P('dp', 'section', None, None, 'tensor')
- proj_grad: bfloat16 [4, 8192, 1024], P('section', 'dp', 'tensor')
All inputs are finite; a program needn't handle non-finite values.
Results may differ from a plain program's by a relative error of at most 0.013.
Values may be sent and summed in bfloat16 or wider, within the bound.
A program may use at most 64 MiB of HBM per device.

v0:
```python
import jax
import jax.numpy as jnp
from jax import lax
from jax.sharding import PartitionSpec as P


def from_behind(value, axis, steps):
    count = lax.axis_size(axis)
    pairs = [(source, (source + steps) % count) for source in range(count)]
    return lax.ppermute(value, axis, pairs)


def per_device(sent_cot, saved_heads, out_proj):
    local_cot = sent_cot[0, 0]
    head_rows = saved_heads[0, 0]
    weight = out_proj[0]
    from_above = from_behind(local_cot[0], "section", -1)
    from_below = from_behind(local_cot[1], "section", 1)
    incoming = jnp.stack([from_above, from_below])
    portion = lax.all_gather(incoming, "tensor", axis=1, tiled=True)
    grad_total = jnp.einsum("rkd,rkh->dh", portion, head_rows, preferred_element_type=jnp.float32)
    head_piece = jnp.einsum("rkd,dh->rkh", portion, weight, preferred_element_type=jnp.float32)
    head_total = head_piece
    grad_total, head_total = (grad_total, head_total)
    rounded = grad_total.astype(jnp.bfloat16).astype(jnp.float32)
    proj_share = lax.psum_scatter(
        rounded.astype(jnp.bfloat16), "dp", scatter_dimension=0, tiled=True
    )
    head_out = head_total.astype(jnp.bfloat16)
    return (head_out[None, None], proj_share[None])


def solution(mesh):
    return jax.shard_map(
        per_device,
        mesh=mesh,
        in_specs=(
            P("dp", "section", None, "tensor", None),
            P("dp", "section", None, None, "tensor"),
            P("section", None, "tensor"),
        ),
        out_specs=(P("dp", "section", None, None, "tensor"), P("section", "dp", "tensor")),
        check_vma=False,
    )
```

profile of v0, /device:TPU:1, one launch (start us, length us, event | category | flops | bytes accessed | tf_op | source)
XLA Modules:
  0.0 128.7 jit_solution(666977936013127331)
XLA Ops:
  7.2 0.0 copy-start
  7.2 0.0 all-gather.2.cloned.1.call-start
  7.2 2.1 %fusion.16 = (bf16[1,1,1,14,8192]{4,2,3,1,0:T(2,128)(2,1)S(1)}, bf16[1,1,1,14,8192]{4,2,3,1,0:T(2,128)(2,1)S(1)}) fusion(bf16[1,1,2,14,8192]{4,2,3,1,0:T(2,128)(2,1)} %param.3), kind=kLoop, calls=%fused_computation.12 | loop fusion | bytes 917504 | tf_op jit(solution)/shard_map/slice | solution.py:17
  9.3 0.3 copy.28
  9.6 2.7 %collective-permute-start.1 = (bf16[14,8192]{1,0:T(8,128)(2,1)S(1)}, bf16[14,8192]{1,0:T(8,128)(2,1)S(1)}, u32[]{:S(2)}, u32[]{:S(2)}) collective-permute-start(bf16[14,8192]{1,0:T(8,128)(2,1)S(1)} %bitcast.27), channel_id=1, source_target_pairs={{0,4},{4,8},{8,12},{12,0},{1,5},{5,9},{9,13},{13,1},{2,6},{6,10},{... | collective-permute-start | bytes 688136 | tf_op jit(solution)/shard_map/ppermute | solution.py:10
  12.3 0.2 copy.29
  12.5 0.1 collective-permute-start
  12.6 5.5 %collective-permute-done.1 = bf16[14,8192]{1,0:T(8,128)(2,1)S(1)} collective-permute-done((bf16[14,8192]{1,0:T(8,128)(2,1)S(1)}, bf16[14,8192]{1,0:T(8,128)(2,1)S(1)}, u32[]{:S(2)}, u32[]{:S(2)}) %collective-permute-start.1) | collective-permute-done | bytes 229408 | tf_op jit(solution)/shard_map/ppermute | solution.py:10
  18.0 0.3 collective-permute-done
  18.4 0.1 pad_maximum_fusion
  18.4 1.2 copy.13
  19.7 0.0 all-gather.2.cloned.1.call-update
  19.7 0.0 reduce-scatter.2.cloned.1.call-start
  19.8 43.0 %all-gather.2.cloned.1.call-done = bf16[2,56,8192]{2,0,1:T(2,128)(2,1)} async-done(((bf16[2,14,8192]{2,0,1:T(2,128)(2,1)}), bf16[2,56,8192]{2,0,1:T(2,128)(2,1)}) %all-gather.2.cloned.1.call-update) | async-done | bytes 1835024 | tf_op jit(solution)/shard_map/all_gather | solution.py:20
  62.7 0.0 copy-done
  62.7 5.8 %fusion = bf16[8192,256]{1,0:T(8,128)(2,1)} fusion(bf16[2,56,8192]{2,0,1:T(2,128)(2,1)} %all-gather.2.cloned.1.call-done, bf16[1,1,2,56,256]{4,3,2,1,0:T(8,128)(2,1)S(1)} %copy-done), kind=kOutput, calls=%fused_computation.1 | convolution fusion | flops 471859200 | bytes 6086656 | tf_op jit(solution)/shard_map/rkd,rkh->dh/dot_general | solution.py:21
  68.5 0.0 copy-start.1
  68.5 0.0 reduce-scatter.2.cloned.1.call-update
  68.5 1.5 %copy-done.1 = bf16[2,56,8192]{2,0,1:T(2,128)(2,1)S(1)} copy-done((bf16[2,56,8192]{2,0,1:T(2,128)(2,1)S(1)}, bf16[2,56,8192]{2,0,1:T(2,128)(2,1)}, u32[]{:S(2)}) %copy-start.1) | copy-done | bytes 1835032
  70.0 5.3 %fusion.10 = bf16[1,1,2,56,256]{4,3,2,1,0:T(8,128)(2,1)} fusion(bf16[1,8192,256]{2,1,0:T(8,128)(2,1)} %param.5, bf16[2,56,8192]{2,0,1:T(2,128)(2,1)S(1)} %copy-done.1), kind=kOutput, calls=%fused_computation.7 | convolution fusion | flops 469790720 | bytes 6086656 | tf_op jit(solution)/shard_map/rkd,dh->rkh/dot_general | solution.py:22
  75.2 46.6 %reduce-scatter.2.cloned.1.call-done = bf16[4096,256]{1,0:T(8,128)(2,1)} async-done(((bf16[8192,256]{1,0:T(8,128)(2,1)}), bf16[4096,256]{1,0:T(8,128)(2,1)}) %reduce-scatter.2.cloned.1.call-update) | async-done | bytes 2097168 | tf_op jit(solution)/shard_map/reduce_scatter | solution.py:26
Async XLA Ops:
  7.2 55.5 %copy-start = (bf16[1,1,2,56,256]{4,3,2,1,0:T(8,128)(2,1)S(1)}, bf16[1,1,2,56,256]{4,3,2,1,0:T(8,128)(2,1)}, u32[]{:S(2)}) copy-start(bf16[1,1,2,56,256]{4,3,2,1,0:T(8,128)(2,1)} %param.4) | copy-start | bytes 172036
  7.2 55.5 %all-gather.2.cloned.1.call-start = ((), (), s32[]{:S(2)}) async-start(), calls=%async_computation.1 | async-start | bytes 2293760 | tf_op jit(solution)/shard_map/all_gather | solution.py:20
  9.6 8.4 %collective-permute-start.1 = (bf16[14,8192]{1,0:T(8,128)(2,1)S(1)}, bf16[14,8192]{1,0:T(8,128)(2,1)S(1)}, u32[]{:S(2)}, u32[]{:S(2)}) collective-permute-start(bf16[14,8192]{1,0:T(8,128)(2,1)S(1)} %bitcast.27), channel_id=1, source_target_pairs={{0,4},{4,8},{8,12},{12,0},{1,5},{5,9},{9,13},{13,1},{2,6},{6,10},{... | collective-permute-start | bytes 688136 | tf_op jit(solution)/shard_map/ppermute | solution.py:10
  12.5 5.8 %collective-permute-start = (bf16[14,8192]{1,0:T(8,128)(2,1)S(1)}, bf16[14,8192]{1,0:T(8,128)(2,1)S(1)}, u32[]{:S(2)}, u32[]{:S(2)}) collective-permute-start(bf16[14,8192]{1,0:T(8,128)(2,1)S(1)} %bitcast.29), channel_id=1, source_target_pairs={{0,12},{4,0},{8,4},{12,8},{1,13},{5,1},{9,5},{13,9},{2,14},{6,2},{... | collective-permute-start | bytes 688136 | tf_op jit(solution)/shard_map/ppermute | solution.py:10
  19.7 102.1 %reduce-scatter.2.cloned.1.call-start = ((), (), s32[]{:S(2)}) async-start(), calls=%async_computation.2 | async-start | bytes 6291456 | tf_op jit(solution)/shard_map/reduce_scatter | solution.py:26
  68.5 1.5 %copy-start.1 = (bf16[2,56,8192]{2,0,1:T(2,128)(2,1)S(1)}, bf16[2,56,8192]{2,0,1:T(2,128)(2,1)}, u32[]{:S(2)}) copy-start(bf16[2,56,8192]{2,0,1:T(2,128)(2,1)} %all-gather.2.cloned.1.call-done) | copy-start | bytes 5505028
Sparse Core Ops, SparseCore 0:
  19.8 42.8 all-gather.1
  68.6 53.1 reduce-scatter.1
where the time goes:
time: 130 us; the launch traced here: 129 us
  waiting for transfers between devices  95.4 us (73%)
  between operations  14.1 us (11%)
  matrix products  11 us (8%)
  local copies, waits for them, and re-layouts  5.34 us (4%)
  starting transfers between devices  2.79 us (2%)
    reduce_scatter x1, waiting for transfers between devices, per_device(): lax.psum_scatter(rounded.astype(jnp.bfloat16), 'dp', scatter_dimension=0,...  46.6 us
    all_gather x1, waiting for transfers between devices, per_device(): portion = lax.all_gather(incoming, 'tensor', axis=1, tiled=True)  43 us
    ppermute x2, waiting for transfers between devices, from_behind(): return lax.ppermute(value, axis, pairs)  5.78 us
    dot_general x1, matrix products, per_device(): jnp.einsum('rkd,rkh->dh', portion, head_rows, preferred_element_type=jnp....  5.76 us
    dot_general x1, matrix products, per_device(): jnp.einsum('rkd,dh->rkh', portion, weight, preferred_element_type=jnp.flo...  5.27 us
    ppermute x2, starting transfers between devices, from_behind(): return lax.ppermute(value, axis, pairs)  2.71 us
  transfers between devices with their start and end apart: 4, of which 4 were waited for; matrix products, arithmetic and copies ran while one was open for 4% of the time, Pallas kernels for 0%

commit v1 on v0

v1 whole, which is shorter than its diff:
```python
import functools

import jax
import jax.numpy as jnp
from jax import lax
from jax.experimental import pallas as pl
from jax.experimental.pallas import tpu as pltpu
from jax.sharding import PartitionSpec as P

MESH = pl.DeviceIdType.MESH
F32 = jnp.float32
ROWS = 16


def kernel(dims, packed, heads, weight, head_out, proj_out,
           gath, hbuf, hfull, hspare, wbuf, stage, acc, spare, acc_in, hstage,
           s1, r1, s2, r2, hs, hr, xs, xr, loc, outs):
    n_dp, n_sec, n_ten, tiles, width, tokens, parts = dims
    dp, sec, ten = (lax.axis_index(a) for a in ("dp", "section", "tensor"))
    spots = [(0, lax.rem(sec + n_sec - 1, n_sec)), (1, lax.rem(sec + 1, n_sec))]
    others = [lax.rem(dp + k, n_dp) for k in range(1, n_dp)]
    has_left, has_right = ten > 0, ten < n_ten - 1

    own_heads = pltpu.make_async_copy(heads, hbuf.at[dp], loc.at[0])
    own_heads.start()
    rows = width * (tiles + 1)
    load = pltpu.make_async_copy(weight.at[pl.ds(pl.multiple_of(dp * rows, rows), rows)], wbuf, loc.at[1])
    load.start()

    barrier = pltpu.get_barrier_semaphore()
    for h in range(n_dp):
        for _, place in spots:
            pl.semaphore_signal(barrier, inc=1, device_id=(h, place, ten), device_id_type=MESH)
    for h in others:
        pl.semaphore_signal(barrier, inc=1, device_id=(h, sec, ten), device_id_type=MESH)

    @pl.when(has_left)
    def _():
        pl.semaphore_signal(barrier, inc=1, device_id=(dp, sec, ten - 1), device_id_type=MESH)

    @pl.when(has_right)
    def _():
        pl.semaphore_signal(barrier, inc=1, device_id=(dp, sec, ten + 1), device_id_type=MESH)

    pl.semaphore_wait(barrier, 2 * n_dp + n_dp - 1 + jnp.where(has_left, 1, 0) + jnp.where(has_right, 1, 0))

    def first(k, r, m):
        low, high = parts[m]
        h = lax.rem(dp + k, n_dp)
        cut = pl.ds(low, high - low)
        return pltpu.make_async_remote_copy(
            src_ref=packed.at[h, r, cut], dst_ref=gath.at[ten, dp, r, cut],
            send_sem=s1.at[k, r, m], recv_sem=r1.at[dp, r, m],
            device_id=(h, spots[r][1], ten), device_id_type=MESH)

    def first_arrival(g, r, m):
        low, high = parts[m]
        cut = pl.ds(low, high - low)
        return pltpu.make_async_remote_copy(
            src_ref=packed.at[0, r, cut], dst_ref=gath.at[ten, g, r, cut],
            send_sem=s1.at[0, r, m], recv_sem=r1.at[g, r, m],
            device_id=(dp, spots[r][1], ten), device_id_type=MESH)

    def hop(item, g, m, step):
        low, high = parts[m]
        block = gath.at[item, g, :, pl.ds(low, high - low)]
        return pltpu.make_async_remote_copy(
            src_ref=block, dst_ref=block,
            send_sem=s2.at[(step + 1) // 2, item, g, m], recv_sem=r2.at[item, g, m],
            device_id=(dp, sec, ten + step), device_id_type=MESH)

    for m in range(len(parts)):
        for k in range(n_dp):
            for r in range(2):
                first(k, r, m).start()
    own_heads.wait()

    def head_copy(k):
        return pltpu.make_async_remote_copy(
            src_ref=heads, dst_ref=hbuf.at[dp],
            send_sem=hs.at[k - 1], recv_sem=hr.at[dp],
            device_id=(lax.rem(dp + k, n_dp), sec, ten), device_id_type=MESH)

    for k in range(1, n_dp):
        head_copy(k).start()

    for m in range(len(parts)):
        for k in range(n_dp):
            g = lax.rem(dp + k, n_dp)
            for r in range(2):
                first_arrival(g, r, m).wait_recv()

            @pl.when(has_right)
            def _():
                hop(ten, g, m, 1).start()

            @pl.when(has_left)
            def _():
                hop(ten, g, m, -1).start()

    for g in others:
        pltpu.make_async_remote_copy(
            src_ref=heads, dst_ref=hbuf.at[g], send_sem=hs.at[0], recv_sem=hr.at[g],
            device_id=(g, sec, ten), device_id_type=MESH).wait_recv()
    load.wait()
    count = hbuf.shape[1]
    place = lax.rem(lax.broadcasted_iota(jnp.int32, (count, hbuf.shape[2]), 0), ROWS)
    extra = ROWS - tokens
    for g in range(n_dp):
        wide = hbuf[g].astype(F32)
        hfull[g] = jnp.where(place < tokens, wide, 0.0).astype(jnp.bfloat16)
        for c in range(tiles):
            turned = pltpu.roll(wide, tokens - extra * c, 0) if tokens - extra * c else wide
            hspare[g, c] = jnp.where(place >= tokens, turned, 0.0).astype(jnp.bfloat16)
        acc[g] = jnp.zeros(acc.shape[1:], F32)
        spare[g] = jnp.zeros(spare.shape[1:], F32)

    def out_copy(c):
        cut = pl.ds(c * width, width)
        return pltpu.make_async_copy(stage.at[cut], proj_out.at[cut], outs.at[c])

    def tile_products(c):
        total = None
        last_rows = wbuf[tiles * width:(tiles + 1) * width]
        for g in range(n_dp):
            block = gath[:, g, :, c].reshape(count, width)
            term = lax.dot_general(block, hfull[g], (((0,), (0,)), ((), ())), preferred_element_type=F32)
            term = term.astype(jnp.bfloat16).astype(F32)
            total = term if total is None else total + term
            spare[g] += lax.dot_general(block, hspare[g, c], (((0,), (0,)), ((), ())), preferred_element_type=F32)
            head = jnp.dot(block, wbuf[c * width:(c + 1) * width], preferred_element_type=F32)
            tail = jnp.dot(block, last_rows, preferred_element_type=F32)
            back = count - (tokens - extra * c)
            tail = pltpu.roll(tail, back, 0) if back != count else tail
            mine = (place >= extra * c) & (place < extra * (c + 1))
            acc[g] += head + jnp.where(mine, tail, 0.0)
        stage[c * width:(c + 1) * width] = total.astype(jnp.bfloat16)
        out_copy(c).start()

    def pass_on(d, m):
        for k in range(n_dp - 1, -1, -1):
            g = lax.rem(dp + k, n_dp)

            @pl.when(ten - d >= 0)
            def _():
                hop(ten - d, g, m, 1).wait_recv()

                @pl.when(has_right)
                def _():
                    hop(ten - d, g, m, 1).start()

            @pl.when(ten + d < n_ten)
            def _():
                hop(ten + d, g, m, -1).wait_recv()

                @pl.when(has_left)
                def _():
                    hop(ten + d, g, m, -1).start()

    def middle(d, carry):
        for m in range(len(parts)):
            pass_on(d, m)
        return carry

    lax.fori_loop(1, n_ten - 1, middle, 0)
    for m, (low, high) in enumerate(parts):
        pass_on(n_ten - 1, m)
        for c in range(low, high):
            tile_products(c)

    def swap(k):
        g = lax.rem(dp + k, n_dp)
        return pltpu.make_async_remote_copy(
            src_ref=acc.at[g], dst_ref=acc_in.at[dp],
            send_sem=xs.at[k - 1], recv_sem=xr.at[dp],
            device_id=(g, sec, ten), device_id_type=MESH)

    for k in range(1, n_dp):
        swap(k).start()
    total = None
    for g in range(n_dp):
        term = spare[g].astype(jnp.bfloat16).astype(F32)
        total = term if total is None else total + term
    stage[tiles * width:(tiles + 1) * width] = total.astype(jnp.bfloat16)
    out_copy(tiles).start()

    for m in range(len(parts)):
        for k in range(n_dp):
            for r in range(2):
                first(k, r, m).wait_send()
    for k in range(1, n_dp):
        head_copy(k).wait_send()

    def drain(item, carry):
        for m in range(len(parts)):
            for g in range(n_dp):
                @pl.when(has_right & (item <= ten))
                def _():
                    hop(item, g, m, 1).wait_send()

                @pl.when(has_left & (item >= ten))
                def _():
                    hop(item, g, m, -1).wait_send()
        return carry

    lax.fori_loop(0, n_ten, drain, 0)

    result = acc[dp]
    for g in others:
        pltpu.make_async_remote_copy(
            src_ref=acc.at[g], dst_ref=acc_in.at[g], send_sem=xs.at[0], recv_sem=xr.at[g],
            device_id=(g, sec, ten), device_id_type=MESH).wait_recv()
        result = result + acc_in[g]
    hstage[...] = result.astype(jnp.bfloat16)
    store = pltpu.make_async_copy(hstage, head_out, loc.at[2])
    store.start()
    for k in range(1, n_dp):
        swap(k).wait_send()
    for c in range(tiles + 1):
        out_copy(c).wait()
    store.wait()


def per_device(mesh, sent_cot, saved_heads, out_proj):
    n_dp, n_sec, n_ten = (mesh.shape[a] for a in ("dp", "section", "tensor"))
    cot, heads, weight = sent_cot[0, 0], saved_heads[0, 0], out_proj[0]
    tokens, depth = cot.shape[1:]
    feats = weight.shape[1]
    extra = ROWS - tokens
    tiles = tokens // extra
    width = depth // n_dp // (tiles + 1)
    cut = cot.reshape(2, tokens, n_dp, tiles + 1, width).transpose(2, 0, 3, 1, 4)
    packed = jnp.concatenate(
        [cut[:, :, :tiles], cut[:, :, tiles].reshape(n_dp, 2, tiles, extra, width)], axis=3)
    blocks = heads.reshape(2, n_ten, tokens, feats).transpose(1, 0, 2, 3)
    count = n_ten * 2 * ROWS
    blocks = jnp.pad(blocks, ((0, 0), (0, 0), (0, extra), (0, 0))).reshape(count, feats)
    parts = ((0, 2), (2, 4), (4, 6), (6, 7)) if tiles == 7 else tuple((c, c + 1) for c in range(tiles))
    n_parts = len(parts)
    dims = (n_dp, n_sec, n_ten, tiles, width, tokens, parts)
    rows = depth // n_dp
    dma = pltpu.SemaphoreType.DMA
    head_out, proj = pl.pallas_call(
        functools.partial(kernel, dims),
        out_shape=(jax.ShapeDtypeStruct((count, feats), jnp.bfloat16),
                   jax.ShapeDtypeStruct((rows, feats), jnp.bfloat16)),
        in_specs=[pl.BlockSpec(memory_space=pl.ANY)] * 3,
        out_specs=(pl.BlockSpec(memory_space=pl.ANY),) * 2,
        scratch_shapes=[
            pltpu.VMEM((n_ten, n_dp, 2, tiles, ROWS, width), jnp.bfloat16),
            pltpu.VMEM((n_dp, count, feats), jnp.bfloat16),
            pltpu.VMEM((n_dp, count, feats), jnp.bfloat16),
            pltpu.VMEM((n_dp, tiles, count, feats), jnp.bfloat16),
            pltpu.VMEM((rows, feats), jnp.bfloat16),
            pltpu.VMEM((rows, feats), jnp.bfloat16),
            pltpu.VMEM((n_dp, count, feats), F32),
            pltpu.VMEM((n_dp, width, feats), F32),
            pltpu.VMEM((n_dp, count, feats), F32),
            pltpu.VMEM((count, feats), jnp.bfloat16),
            dma((n_dp, 2, n_parts)), dma((n_dp, 2, n_parts)),
            dma((2, n_ten, n_dp, n_parts)), dma((n_ten, n_dp, n_parts)),
            dma((n_dp,)), dma((n_dp,)), dma((n_dp,)), dma((n_dp,)),
            dma((3,)), dma((tiles + 1,)),
        ],
        compiler_params=pltpu.CompilerParams(
            collective_id=0, has_side_effects=True, vmem_limit_bytes=48 * 2**20),
        name="relay_grads",
    )(packed, blocks, weight)
    head = head_out.reshape(n_ten, 2, ROWS, feats)[:, :, :tokens].transpose(1, 0, 2, 3)
    return head.reshape(1, 1, 2, n_ten * tokens, feats), proj[None]


def solution(mesh):
    return jax.shard_map(
        functools.partial(per_device, mesh),
        mesh=mesh,
        in_specs=(
            P("dp", "section", None, "tensor", None),
            P("dp", "section", None, None, "tensor"),
            P("section", None, "tensor"),
        ),
        out_specs=(P("dp", "section", None, None, "tensor"), P("section", "dp", "tensor")),
        check_vma=False,
    )
```

time: 130 us -> 51 us (0.39)
  waiting for transfers between devices: 95.4 us -> 0 us
  Pallas kernels: 0 us -> 45 us
  between operations: 14.1 us -> 0.71 us
  matrix products: 11 us -> 0 us
  starting transfers between devices: 2.79 us -> 0 us
    reduce_scatter x1 -> x0, waiting for transfers between devices: 46.6 us -> none  [per_device(): lax.psum_scatter(rounded.astype(jnp.bfloat16), 'dp', scatter_dimension=0,...]
    pallas_call x0 -> x1, Pallas kernels: none -> 45 us  [per_device(): pl.pallas_call(functools.partial(kernel, dims), out_shape=(jax.ShapeDtype...]
    all_gather x1 -> x0, waiting for transfers between devices: 43 us -> none  [per_device(): portion = lax.all_gather(incoming, 'tensor', axis=1, tiled=True)]
    dot_general x2 -> x0, matrix products: 11 us -> none  [the longest x1 5.76 us: per_device(): jnp.einsum('rkd,rkh->dh', portion, head_rows, preferred_element_type=jnp....]
    ppermute x2 -> x0, waiting for transfers between devices: 5.78 us -> none  [from_behind(): return lax.ppermute(value, axis, pairs)]
    ppermute x2 -> x0, starting transfers between devices: 2.71 us -> none  [from_behind(): return lax.ppermute(value, axis, pairs)]
    slice x1 -> x3, local copies, waits for them, and re-layouts: 2.11 us -> 0.1 us  [the longest x2 0.07 us: per_device(): cut[:, :, tiles].reshape(n_dp, 2, tiles, extra, width)]
    unnamed x6 -> x5, local copies, waits for them, and re-layouts: 1.99 us -> 2.87 us
  transfers between devices with their start and end apart: 4 -> 0, of which waited for: 4 -> 0; matrix products, arithmetic and copies ran while one was open for 4% -> 0% of each run, Pallas kernels for 0% -> 0%
where the time goes in v1:
time: 51 us; the launch traced here: 50.5 us
  Pallas kernels  45 us (88%)
  local copies, waits for them, and re-layouts  4.62 us (9%)
  between operations  0.71 us (1%)
    pallas_call x1, Pallas kernels, per_device(): pl.pallas_call(functools.partial(kernel, dims), out_shape=(jax.ShapeDtype...  45 us
    unnamed x5, local copies, waits for them, and re-layouts  2.87 us
    another operation x2, local copies, waits for them, and re-layouts, per_device(): cot.reshape(2, tokens, n_dp, tiles + 1, width).transpose(2, 0, 3, 1, 4)  1.59 us

profile of v1, /device:TPU:1, one launch (start us, length us, event | category | flops | bytes accessed | tf_op | source)
XLA Modules:
  0.0 50.5 jit_solution(13643206068303268830)
XLA Ops:
  0.6 0.9 %copy.10 = bf16[1,1,2,56,256]{4,2,3,1,0:T(2,128)(2,1)S(1)} copy(bf16[1,1,2,56,256]{4,3,2,1,0:T(8,128)(2,1)} %param.4) | data formatting | bytes 114688 | tf_op args[1]
  1.5 1.3 %reshape_squeeze.9 = bf16[2,14,2,8,512]{4,3,2,0,1:T(8,128)(2,1)S(1)} reshape(bf16[1,1,2,14,8192]{4,2,3,1,0:T(2,128)(2,1)} %param.3) | data formatting | bytes 917504 | tf_op jit(solution)/shard_map/reshape;squeeze | solution.py:232
  2.9 0.3 copy.17
  3.2 0.1 copy.8
  3.3 0.1 pad_maximum_fusion.packed
  3.4 45.0 %relay_grads.1 = (bf16[128,256]{1,0:T(8,128)(2,1)S(1)}, bf16[4096,256]{1,0:T(8,128)(2,1)S(1)}) custom-call(bf16[2,2,7,16,512]{4,3,2,1,0:T(8,128)(2,1)S(1)} %pad_maximum_fusion.packed, bf16[128,256]{1,0:T(8,128)(2,1)S(1)} %bitcast.18, bf16[8192,256]{1,0:T(8,128)(2,1)} %bitcast.20), custom_call_target="tpu_custom_call" | custom-call | tf_op jit(solution)/shard_map/relay_grads/pallas_call | solution.py:243
  48.5 0.6 %copy.13 = bf16[1,1,2,56,256]{4,3,2,1,0:T(8,128)(2,1)} copy(bf16[1,1,2,56,256]{4,2,3,1,0:T(2,128)(2,1)S(1)} %bitcast.24) | data formatting | bytes 114688
  49.2 1.3 %copy.19 = bf16[1,4096,256]{2,1,0:T(8,128)(2,1)} copy(bf16[1,4096,256]{2,1,0:T(8,128)(2,1)S(1)} %bitcast.17) | data formatting | bytes 4194304
  (6 shorter events, 0.1 us)

commit v2 on v1

--- a/solution.py
+++ b/solution.py
@@ -13,7 +13,7 @@
 
 
 def kernel(dims, packed, heads, weight, head_out, proj_out,
-           gath, hbuf, hfull, hspare, wbuf, stage, acc, spare, acc_in, hstage,
+           gath, hbuf, hwide, hfull, hspare, wbuf, stage, part, acc, spare, acc_in, hstage,
            s1, r1, s2, r2, hs, hr, xs, xr, loc, outs):
     n_dp, n_sec, n_ten, tiles, width, tokens, parts = dims
     dp, sec, ten = (lax.axis_index(a) for a in ("dp", "section", "tensor"))
@@ -21,12 +21,6 @@
     others = [lax.rem(dp + k, n_dp) for k in range(1, n_dp)]
     has_left, has_right = ten > 0, ten < n_ten - 1
 
-    own_heads = pltpu.make_async_copy(heads, hbuf.at[dp], loc.at[0])
-    own_heads.start()
-    rows = width * (tiles + 1)
-    load = pltpu.make_async_copy(weight.at[pl.ds(pl.multiple_of(dp * rows, rows), rows)], wbuf, loc.at[1])
-    load.start()
-
     barrier = pltpu.get_barrier_semaphore()
     for h in range(n_dp):
         for _, place in spots:
@@ -42,6 +36,12 @@
     def _():
         pl.semaphore_signal(barrier, inc=1, device_id=(dp, sec, ten + 1), device_id_type=MESH)
 
+    own_heads = pltpu.make_async_copy(heads, hbuf.at[dp], loc.at[0])
+    own_heads.start()
+    rows = width * (tiles + 1)
+    load = pltpu.make_async_copy(weight.at[pl.ds(pl.multiple_of(dp * rows, rows), rows)], wbuf, loc.at[1])
+    load.start()
+
     pl.semaphore_wait(barrier, 2 * n_dp + n_dp - 1 + jnp.where(has_left, 1, 0) + jnp.where(has_right, 1, 0))
 
     def first(k, r, m):
@@ -103,11 +103,18 @@
             src_ref=heads, dst_ref=hbuf.at[g], send_sem=hs.at[0], recv_sem=hr.at[g],
             device_id=(g, sec, ten), device_id_type=MESH).wait_recv()
     load.wait()
-    count = hbuf.shape[1]
-    place = lax.rem(lax.broadcasted_iota(jnp.int32, (count, hbuf.shape[2]), 0), ROWS)
+    count, feats = hwide.shape
+    place = lax.rem(lax.broadcasted_iota(jnp.int32, (count, feats), 0), ROWS)
+    length = n_ten * tokens
     extra = ROWS - tokens
     for g in range(n_dp):
-        wide = hbuf[g].astype(F32)
+        for r in range(2):
+            lines = hbuf[g, r].astype(F32)
+            for t in range(n_ten):
+                turned = pltpu.roll(lines, length - t * tokens, 0) if t else lines
+                at = (2 * t + r) * ROWS
+                hwide[at:at + ROWS] = turned[:ROWS]
+        wide = hwide[...]
         hfull[g] = jnp.where(place < tokens, wide, 0.0).astype(jnp.bfloat16)
         for c in range(tiles):
             turned = pltpu.roll(wide, tokens - extra * c, 0) if tokens - extra * c else wide
@@ -119,54 +126,37 @@
         cut = pl.ds(c * width, width)
         return pltpu.make_async_copy(stage.at[cut], proj_out.at[cut], outs.at[c])
 
-    def tile_products(c):
-        total = None
-        last_rows = wbuf[tiles * width:(tiles + 1) * width]
-        for g in range(n_dp):
-            block = gath[:, g, :, c].reshape(count, width)
-            term = lax.dot_general(block, hfull[g], (((0,), (0,)), ((), ())), preferred_element_type=F32)
-            term = term.astype(jnp.bfloat16).astype(F32)
-            total = term if total is None else total + term
-            spare[g] += lax.dot_general(block, hspare[g, c], (((0,), (0,)), ((), ())), preferred_element_type=F32)
-            head = jnp.dot(block, wbuf[c * width:(c + 1) * width], preferred_element_type=F32)
-            tail = jnp.dot(block, last_rows, preferred_element_type=F32)
-            back = count - (tokens - extra * c)
-            tail = pltpu.roll(tail, back, 0) if back != count else tail
-            mine = (place >= extra * c) & (place < extra * (c + 1))
-            acc[g] += head + jnp.where(mine, tail, 0.0)
-        stage[c * width:(c + 1) * width] = total.astype(jnp.bfloat16)
-        out_copy(c).start()
-
-    def pass_on(d, m):
-        for k in range(n_dp - 1, -1, -1):
-            g = lax.rem(dp + k, n_dp)
-
-            @pl.when(ten - d >= 0)
-            def _():
-                hop(ten - d, g, m, 1).wait_recv()
-
-                @pl.when(has_right)
-                def _():
-                    hop(ten - d, g, m, 1).start()
-
-            @pl.when(ten + d < n_ten)
-            def _():
-                hop(ten + d, g, m, -1).wait_recv()
-
-                @pl.when(has_left)
-                def _():
-                    hop(ten + d, g, m, -1).start()
-
-    def middle(d, carry):
-        for m in range(len(parts)):
-            pass_on(d, m)
-        return carry
-
-    lax.fori_loop(1, n_ten - 1, middle, 0)
-    for m, (low, high) in enumerate(parts):
-        pass_on(n_ten - 1, m)
-        for c in range(low, high):
-            tile_products(c)
+    def tile_term(g, c):
+        block = gath[:, g, :, c].reshape(count, width)
+        term = lax.dot_general(block, hfull[g], (((0,), (0,)), ((), ())), preferred_element_type=F32)
+        spare[g] += lax.dot_general(block, hspare[g, c], (((0,), (0,)), ((), ())), preferred_element_type=F32)
+        head = jnp.dot(block, wbuf[c * width:(c + 1) * width], preferred_element_type=F32)
+        tail = jnp.dot(block, wbuf[tiles * width:(tiles + 1) * width], preferred_element_type=F32)
+        back = count - (tokens - extra * c)
+        tail = pltpu.roll(tail, back, 0) if back != count else tail
+        mine = (place >= extra * c) & (place < extra * (c + 1))
+        acc[g] += head + jnp.where(mine, tail, 0.0)
+        return term.astype(jnp.bfloat16).astype(F32)
+
+    def sum_others(terms):
+        return functools.reduce(lambda a, b: a + b, terms)
+
+    def pass_on(d, g, m):
+        @pl.when(ten - d >= 0)
+        def _():
+            hop(ten - d, g, m, 1).wait_recv()
+
+            @pl.when(has_right)
+            def _():
+                hop(ten - d, g, m, 1).start()
+
+        @pl.when(ten + d < n_ten)
+        def _():
+            hop(ten + d, g, m, -1).wait_recv()
+
+            @pl.when(has_left)
+            def _():
+                hop(ten + d, g, m, -1).start()
 
     def swap(k):
         g = lax.rem(dp + k, n_dp)
@@ -175,13 +165,30 @@
             send_sem=xs.at[k - 1], recv_sem=xr.at[dp],
             device_id=(g, sec, ten), device_id_type=MESH)
 
+    def middle(d, carry):
+        for g in others + [dp]:
+            for m in range(len(parts)):
+                pass_on(d, g, m)
+        return carry
+
+    lax.fori_loop(1, n_ten - 1, middle, 0)
+    for m, (low, high) in enumerate(parts):
+        for g in others:
+            pass_on(n_ten - 1, g, m)
+        for c in range(low, high):
+            part[c * width:(c + 1) * width] = sum_others([tile_term(g, c) for g in others])
     for k in range(1, n_dp):
         swap(k).start()
-    total = None
-    for g in range(n_dp):
-        term = spare[g].astype(jnp.bfloat16).astype(F32)
-        total = term if total is None else total + term
-    stage[tiles * width:(tiles + 1) * width] = total.astype(jnp.bfloat16)
+    part[tiles * width:] = sum_others([spare[g].astype(jnp.bfloat16).astype(F32) for g in others])
+    for m, (low, high) in enumerate(parts):
+        pass_on(n_ten - 1, dp, m)
+        for c in range(low, high):
+            cut = slice(c * width, (c + 1) * width)
+            stage[cut] = (part[cut] + tile_term(dp, c)).astype(jnp.bfloat16)
+            out_copy(c).start()
+
+    own = spare[dp].astype(jnp.bfloat16).astype(F32)
+    stage[tiles * width:] = (part[tiles * width:] + own).astype(jnp.bfloat16)
     out_copy(tiles).start()
 
     for m in range(len(parts)):
@@ -232,9 +239,7 @@
     cut = cot.reshape(2, tokens, n_dp, tiles + 1, width).transpose(2, 0, 3, 1, 4)
     packed = jnp.concatenate(
         [cut[:, :, :tiles], cut[:, :, tiles].reshape(n_dp, 2, tiles, extra, width)], axis=3)
-    blocks = heads.reshape(2, n_ten, tokens, feats).transpose(1, 0, 2, 3)
     count = n_ten * 2 * ROWS
-    blocks = jnp.pad(blocks, ((0, 0), (0, 0), (0, extra), (0, 0))).reshape(count, feats)
     parts = ((0, 2), (2, 4), (4, 6), (6, 7)) if tiles == 7 else tuple((c, c + 1) for c in range(tiles))
     n_parts = len(parts)
     dims = (n_dp, n_sec, n_ten, tiles, width, tokens, parts)
@@ -248,11 +253,13 @@
         out_specs=(pl.BlockSpec(memory_space=pl.ANY),) * 2,
         scratch_shapes=[
             pltpu.VMEM((n_ten, n_dp, 2, tiles, ROWS, width), jnp.bfloat16),
-            pltpu.VMEM((n_dp, count, feats), jnp.bfloat16),
+            pltpu.VMEM((n_dp,) + heads.shape, jnp.bfloat16),
+            pltpu.VMEM((count, feats), F32),
             pltpu.VMEM((n_dp, count, feats), jnp.bfloat16),
             pltpu.VMEM((n_dp, tiles, count, feats), jnp.bfloat16),
             pltpu.VMEM((rows, feats), jnp.bfloat16),
             pltpu.VMEM((rows, feats), jnp.bfloat16),
+            pltpu.VMEM((rows, feats), F32),
             pltpu.VMEM((n_dp, count, feats), F32),
             pltpu.VMEM((n_dp, width, feats), F32),
             pltpu.VMEM((n_dp, count, feats), F32),
@@ -265,7 +272,7 @@
         compiler_params=pltpu.CompilerParams(
             collective_id=0, has_side_effects=True, vmem_limit_bytes=48 * 2**20),
         name="relay_grads",
-    )(packed, blocks, weight)
+    )(packed, heads, weight)
     head = head_out.reshape(n_ten, 2, ROWS, feats)[:, :, :tokens].transpose(1, 0, 2, 3)
     return head.reshape(1, 1, 2, n_ten * tokens, feats), proj[None]
 

time: 51 us -> 45.4 us (0.89)
  Pallas kernels: 45 us -> 40.6 us
  local copies, waits for them, and re-layouts: 4.62 us -> 3.75 us
    pallas_call x1, Pallas kernels: 45 us -> 40.6 us  [per_device(): pl.pallas_call(functools.partial(kernel, dims), out_shape=(jax.ShapeDtype...]
    unnamed x5, local copies, waits for them, and re-layouts: 2.87 us -> 2 us
where the time goes in v2:
time: 45.4 us; the launch traced here: 45.2 us
  Pallas kernels  40.6 us (89%)
  local copies, waits for them, and re-layouts  3.75 us (8%)
  between operations  0.71 us (2%)
    pallas_call x1, Pallas kernels, per_device(): pl.pallas_call(functools.partial(kernel, dims), out_shape=(jax.ShapeDtype...  40.6 us
    unnamed x5, local copies, waits for them, and re-layouts  2 us
    another operation x2, local copies, waits for them, and re-layouts, per_device(): cot.reshape(2, tokens, n_dp, tiles + 1, width).transpose(2, 0, 3, 1, 4)  1.61 us

profile of v2, /device:TPU:1, one launch (start us, length us, event | category | flops | bytes accessed | tf_op | source)
XLA Modules:
  0.0 45.2 jit_solution(7545953486731406668)
XLA Ops:
  0.6 0.0 copy-start
  0.6 1.3 %reshape_squeeze.6 = bf16[2,14,2,8,512]{4,3,2,0,1:T(8,128)(2,1)S(1)} reshape(bf16[1,1,2,14,8192]{4,2,3,1,0:T(2,128)(2,1)} %param.3) | data formatting | bytes 917504 | tf_op jit(solution)/shard_map/reshape;squeeze | solution.py:239
  2.0 0.3 copy.13
  2.3 0.1 copy.7
  2.4 0.1 pad_maximum_fusion.packed
  2.6 0.0 copy-done
  2.6 40.6 %relay_grads.1 = (bf16[128,256]{1,0:T(8,128)(2,1)S(1)}, bf16[4096,256]{1,0:T(8,128)(2,1)S(1)}) custom-call(bf16[2,2,7,16,512]{4,3,2,1,0:T(8,128)(2,1)S(1)} %pad_maximum_fusion.packed, bf16[2,56,256]{2,1,0:T(8,128)(2,1)S(1)} %bitcast.16, bf16[8192,256]{1,0:T(8,128)(2,1)} %bitcast.17), custom_call_target="tpu_custom_call" | custom-call | tf_op jit(solution)/shard_map/relay_grads/pallas_call | solution.py:248
  43.3 0.6 %copy.10 = bf16[1,1,2,56,256]{4,3,2,1,0:T(8,128)(2,1)} copy(bf16[1,1,2,56,256]{4,2,3,1,0:T(2,128)(2,1)S(1)} %bitcast.21) | data formatting | bytes 114688
  43.9 1.3 %copy.15 = bf16[1,4096,256]{2,1,0:T(8,128)(2,1)} copy(bf16[1,4096,256]{2,1,0:T(8,128)(2,1)S(1)} %bitcast.14) | data formatting | bytes 4194304
  (4 shorter events, 0.1 us)
Async XLA Ops:
  0.6 1.9 %copy-start = (bf16[1,1,2,56,256]{4,3,2,1,0:T(8,128)(2,1)S(1)}, bf16[1,1,2,56,256]{4,3,2,1,0:T(8,128)(2,1)}, u32[]{:S(2)}) copy-start(bf16[1,1,2,56,256]{4,3,2,1,0:T(8,128)(2,1)} %param.4) | copy-start | bytes 172036

commit v3 on v2

--- a/solution.py
+++ b/solution.py
@@ -13,7 +13,7 @@
 
 
 def kernel(dims, packed, heads, weight, head_out, proj_out,
-           gath, hbuf, hwide, hfull, hspare, wbuf, stage, part, acc, spare, acc_in, hstage,
+           gath, hbuf, hwide, hfull, hspare, wbuf, stage, part, acc, spare, acc_in, lines, hstage,
            s1, r1, s2, r2, hs, hr, xs, xr, loc, outs):
     n_dp, n_sec, n_ten, tiles, width, tokens, parts = dims
     dp, sec, ten = (lax.axis_index(a) for a in ("dp", "section", "tensor"))
@@ -109,9 +109,9 @@
     extra = ROWS - tokens
     for g in range(n_dp):
         for r in range(2):
-            lines = hbuf[g, r].astype(F32)
+            rows_r = hbuf[g, r].astype(F32)
             for t in range(n_ten):
-                turned = pltpu.roll(lines, length - t * tokens, 0) if t else lines
+                turned = pltpu.roll(rows_r, length - t * tokens, 0) if t else rows_r
                 at = (2 * t + r) * ROWS
                 hwide[at:at + ROWS] = turned[:ROWS]
         wide = hwide[...]
@@ -128,10 +128,14 @@
 
     def tile_term(g, c):
         block = gath[:, g, :, c].reshape(count, width)
-        term = lax.dot_general(block, hfull[g], (((0,), (0,)), ((), ())), preferred_element_type=F32)
-        spare[g] += lax.dot_general(block, hspare[g, c], (((0,), (0,)), ((), ())), preferred_element_type=F32)
-        head = jnp.dot(block, wbuf[c * width:(c + 1) * width], preferred_element_type=F32)
-        tail = jnp.dot(block, wbuf[tiles * width:(tiles + 1) * width], preferred_element_type=F32)
+        sides = jnp.concatenate([hfull[g], hspare[g, c]], axis=1)
+        both = lax.dot_general(block, sides, (((0,), (0,)), ((), ())), preferred_element_type=F32)
+        term = both[:, :feats]
+        spare[g] += both[:, feats:]
+        sides = jnp.concatenate(
+            [wbuf[c * width:(c + 1) * width], wbuf[tiles * width:(tiles + 1) * width]], axis=1)
+        both = jnp.dot(block, sides, preferred_element_type=F32)
+        head, tail = both[:, :feats], both[:, feats:]
         back = count - (tokens - extra * c)
         tail = pltpu.roll(tail, back, 0) if back != count else tail
         mine = (place >= extra * c) & (place < extra * (c + 1))
@@ -179,6 +183,29 @@
             part[c * width:(c + 1) * width] = sum_others([tile_term(g, c) for g in others])
     for k in range(1, n_dp):
         swap(k).start()
+    for m in range(len(parts)):
+        for k in range(n_dp):
+            for r in range(2):
+                first(k, r, m).wait_send()
+    for k in range(1, n_dp):
+        head_copy(k).wait_send()
+
+    def drain(item, carry):
+        for m in range(len(parts)):
+            for g in range(n_dp):
+                @pl.when(has_right & (item <= ten))
+                def _():
+                    hop(item, g, m, 1).wait_send()
+
+                @pl.when(has_left & (item >= ten))
+                def _():
+                    hop(item, g, m, -1).wait_send()
+        return carry
+
+    @pl.when(jnp.logical_not(has_left & has_right))
+    def _():
+        lax.fori_loop(0, n_ten, drain, 0)
+
     part[tiles * width:] = sum_others([spare[g].astype(jnp.bfloat16).astype(F32) for g in others])
     for m, (low, high) in enumerate(parts):
         pass_on(n_ten - 1, dp, m)
@@ -191,26 +218,9 @@
     stage[tiles * width:] = (part[tiles * width:] + own).astype(jnp.bfloat16)
     out_copy(tiles).start()
 
-    for m in range(len(parts)):
-        for k in range(n_dp):
-            for r in range(2):
-                first(k, r, m).wait_send()
-    for k in range(1, n_dp):
-        head_copy(k).wait_send()
-
-    def drain(item, carry):
-        for m in range(len(parts)):
-            for g in range(n_dp):
-                @pl.when(has_right & (item <= ten))
-                def _():
-                    hop(item, g, m, 1).wait_send()
-
-                @pl.when(has_left & (item >= ten))
-                def _():
-                    hop(item, g, m, -1).wait_send()
-        return carry
-
-    lax.fori_loop(0, n_ten, drain, 0)
+    @pl.when(has_left & has_right)
+    def _():
+        lax.fori_loop(0, n_ten, drain, 0)
 
     result = acc[dp]
     for g in others:
@@ -218,7 +228,11 @@
             src_ref=acc.at[g], dst_ref=acc_in.at[g], send_sem=xs.at[0], recv_sem=xr.at[g],
             device_id=(g, sec, ten), device_id_type=MESH).wait_recv()
         result = result + acc_in[g]
-    hstage[...] = result.astype(jnp.bfloat16)
+    for r in range(2):
+        for t in range(n_ten):
+            at = (2 * t + r) * ROWS
+            lines[r, t * tokens:t * tokens + ROWS] = result[at:at + ROWS]
+        hstage[r] = lines[r, :length].astype(jnp.bfloat16)
     store = pltpu.make_async_copy(hstage, head_out, loc.at[2])
     store.start()
     for k in range(1, n_dp):
@@ -226,6 +240,18 @@
     for c in range(tiles + 1):
         out_copy(c).wait()
     store.wait()
+
+
+def finish(pieces, head, proj, head_out, proj_out, sems):
+    rows = proj.shape[0] // pieces
+    copies = [pltpu.make_async_copy(head, head_out, sems.at[pieces])]
+    for c in range(pieces):
+        cut = pl.ds(c * rows, rows)
+        copies.append(pltpu.make_async_copy(proj.at[cut], proj_out.at[cut], sems.at[c]))
+    for copy in copies:
+        copy.start()
+    for copy in copies:
+        copy.wait()
 
 
 def per_device(mesh, sent_cot, saved_heads, out_proj):
@@ -247,7 +273,7 @@
     dma = pltpu.SemaphoreType.DMA
     head_out, proj = pl.pallas_call(
         functools.partial(kernel, dims),
-        out_shape=(jax.ShapeDtypeStruct((count, feats), jnp.bfloat16),
+        out_shape=(jax.ShapeDtypeStruct(heads.shape, jnp.bfloat16),
                    jax.ShapeDtypeStruct((rows, feats), jnp.bfloat16)),
         in_specs=[pl.BlockSpec(memory_space=pl.ANY)] * 3,
         out_specs=(pl.BlockSpec(memory_space=pl.ANY),) * 2,
@@ -263,7 +289,8 @@
             pltpu.VMEM((n_dp, count, feats), F32),
             pltpu.VMEM((n_dp, width, feats), F32),
             pltpu.VMEM((n_dp, count, feats), F32),
-            pltpu.VMEM((count, feats), jnp.bfloat16),
+            pltpu.VMEM((2, -(-(n_ten * tokens + extra) // 8) * 8, feats), F32),
+            pltpu.VMEM(heads.shape, jnp.bfloat16),
             dma((n_dp, 2, n_parts)), dma((n_dp, 2, n_parts)),
             dma((2, n_ten, n_dp, n_parts)), dma((n_ten, n_dp, n_parts)),
             dma((n_dp,)), dma((n_dp,)), dma((n_dp,)), dma((n_dp,)),
@@ -273,8 +300,17 @@
             collective_id=0, has_side_effects=True, vmem_limit_bytes=48 * 2**20),
         name="relay_grads",
     )(packed, heads, weight)
-    head = head_out.reshape(n_ten, 2, ROWS, feats)[:, :, :tokens].transpose(1, 0, 2, 3)
-    return head.reshape(1, 1, 2, n_ten * tokens, feats), proj[None]
+    head_out, proj = pl.pallas_call(
+        functools.partial(finish, tiles + 1),
+        out_shape=(jax.ShapeDtypeStruct(heads.shape, jnp.bfloat16),
+                   jax.ShapeDtypeStruct((rows, feats), jnp.bfloat16)),
+        in_specs=[pl.BlockSpec(memory_space=pl.ANY)] * 2,
+        out_specs=(pl.BlockSpec(memory_space=pl.ANY),) * 2,
+        scratch_shapes=[dma((tiles + 2,))],
+        compiler_params=pltpu.CompilerParams(vmem_limit_bytes=2**20),
+        name="write_out",
+    )(head_out, proj)
+    return head_out[None, None], proj[None]
 
 
 def solution(mesh):

time: 45.4 us -> 44.6 us (0.982)
  local copies, waits for them, and re-layouts: 3.75 us -> 1.76 us
  Pallas kernels: 40.6 us -> 41.9 us
    unnamed x5 -> x2, local copies, waits for them, and re-layouts: 2 us -> 0.01 us
    pallas_call x0 -> x1, Pallas kernels: none -> 1.4 us  [per_device(): pl.pallas_call(functools.partial(finish, tiles + 1), out_shape=(jax.Shape...]
where the time goes in v3:
time: 44.6 us; the launch traced here: 44.5 us
  Pallas kernels  41.9 us (94%)
  local copies, waits for them, and re-layouts  1.76 us (4%)
  between operations  0.7 us (2%)
    pallas_call x1, Pallas kernels, per_device(): pl.pallas_call(functools.partial(kernel, dims), out_shape=(jax.ShapeDtype...  40.5 us
    another operation x2, local copies, waits for them, and re-layouts, per_device(): cot.reshape(2, tokens, n_dp, tiles + 1, width).transpose(2, 0, 3, 1, 4)  1.61 us
    pallas_call x1, Pallas kernels, per_device(): pl.pallas_call(functools.partial(finish, tiles + 1), out_shape=(jax.Shape...  1.4 us

profile of v3, /device:TPU:1, one launch (start us, length us, event | category | flops | bytes accessed | tf_op | source)
XLA Modules:
  0.0 44.5 jit_solution(12573921132692873078)
XLA Ops:
  0.6 0.0 copy-start
  0.6 1.3 %reshape_squeeze.6 = bf16[2,14,2,8,512]{4,3,2,0,1:T(8,128)(2,1)S(1)} reshape(bf16[1,1,2,14,8192]{4,2,3,1,0:T(2,128)(2,1)} %param.3) | data formatting | bytes 917504 | tf_op jit(solution)/shard_map/reshape;squeeze | solution.py:265
  2.0 0.3 copy.9
  2.3 0.1 copy.6
  2.4 0.1 pad_maximum_fusion.packed
  2.6 0.0 copy-done
  2.6 40.5 %relay_grads.1 = (bf16[2,56,256]{2,1,0:T(8,128)(2,1)S(1)}, bf16[4096,256]{1,0:T(8,128)(2,1)S(1)}) custom-call(bf16[2,2,7,16,512]{4,3,2,1,0:T(8,128)(2,1)S(1)} %pad_maximum_fusion.packed, bf16[2,56,256]{2,1,0:T(8,128)(2,1)S(1)} %bitcast.10, bf16[8192,256]{1,0:T(8,128)(2,1)} %bitcast.11), custom_call_target="tpu_custom_call" | custom-call | tf_op jit(solution)/shard_map/relay_grads/pallas_call | solution.py:274
  43.1 1.4 %write_out.1 = (bf16[2,56,256]{2,1,0:T(8,128)(2,1)}, bf16[4096,256]{1,0:T(8,128)(2,1)}) custom-call(bf16[2,56,256]{2,1,0:T(8,128)(2,1)S(1)} %get-tuple-element.6.head, bf16[4096,256]{1,0:T(8,128)(2,1)S(1)} %get-tuple-element.7.proj), custom_call_target="tpu_custom_call" | custom-call | tf_op jit(solution)/shard_map/write_out/pallas_call | solution.py:303
  (3 shorter events, 0.1 us)
Async XLA Ops:
  0.6 1.9 %copy-start = (bf16[1,1,2,56,256]{4,3,2,1,0:T(8,128)(2,1)S(1)}, bf16[1,1,2,56,256]{4,3,2,1,0:T(8,128)(2,1)}, u32[]{:S(2)}) copy-start(bf16[1,1,2,56,256]{4,3,2,1,0:T(8,128)(2,1)} %param.4) | copy-start | bytes 172036

commit v4 on v3

--- a/solution.py
+++ b/solution.py
@@ -301,12 +301,12 @@
         name="relay_grads",
     )(packed, heads, weight)
     head_out, proj = pl.pallas_call(
-        functools.partial(finish, tiles + 1),
+        functools.partial(finish, 2),
         out_shape=(jax.ShapeDtypeStruct(heads.shape, jnp.bfloat16),
                    jax.ShapeDtypeStruct((rows, feats), jnp.bfloat16)),
         in_specs=[pl.BlockSpec(memory_space=pl.ANY)] * 2,
         out_specs=(pl.BlockSpec(memory_space=pl.ANY),) * 2,
-        scratch_shapes=[dma((tiles + 2,))],
+        scratch_shapes=[dma((2 + 1,))],
         compiler_params=pltpu.CompilerParams(vmem_limit_bytes=2**20),
         name="write_out",
     )(head_out, proj)

time: 44.6 us -> 44.6 us (level)
  no operation moved by 1% of the time
where the time goes in v4:
time: 44.6 us; the launch traced here: 44.4 us
  Pallas kernels  41.9 us (94%)
  local copies, waits for them, and re-layouts  1.76 us (4%)
  between operations  0.7 us (2%)
    pallas_call x1, Pallas kernels, per_device(): pl.pallas_call(functools.partial(kernel, dims), out_shape=(jax.ShapeDtype...  40.5 us
    another operation x2, local copies, waits for them, and re-layouts, per_device(): cot.reshape(2, tokens, n_dp, tiles + 1, width).transpose(2, 0, 3, 1, 4)  1.61 us
    pallas_call x1, Pallas kernels, per_device(): pl.pallas_call(functools.partial(finish, 2), out_shape=(jax.ShapeDtypeStr...  1.36 us

profile of v4, /device:TPU:1, one launch (start us, length us, event | category | flops | bytes accessed | tf_op | source)
XLA Modules:
  0.0 44.4 jit_solution(1145452131345065583)
XLA Ops:
  0.6 0.0 copy-start
  0.6 1.3 %reshape_squeeze.6 = bf16[2,14,2,8,512]{4,3,2,0,1:T(8,128)(2,1)S(1)} reshape(bf16[1,1,2,14,8192]{4,2,3,1,0:T(2,128)(2,1)} %param.3) | data formatting | bytes 917504 | tf_op jit(solution)/shard_map/reshape;squeeze | solution.py:265
  2.0 0.3 copy.9
  2.3 0.1 copy.6
  2.4 0.1 pad_maximum_fusion.packed
  2.6 0.0 copy-done
  2.6 40.5 %relay_grads.1 = (bf16[2,56,256]{2,1,0:T(8,128)(2,1)S(1)}, bf16[4096,256]{1,0:T(8,128)(2,1)S(1)}) custom-call(bf16[2,2,7,16,512]{4,3,2,1,0:T(8,128)(2,1)S(1)} %pad_maximum_fusion.packed, bf16[2,56,256]{2,1,0:T(8,128)(2,1)S(1)} %bitcast.10, bf16[8192,256]{1,0:T(8,128)(2,1)} %bitcast.11), custom_call_target="tpu_custom_call" | custom-call | tf_op jit(solution)/shard_map/relay_grads/pallas_call | solution.py:274
  43.1 1.4 %write_out.1 = (bf16[2,56,256]{2,1,0:T(8,128)(2,1)}, bf16[4096,256]{1,0:T(8,128)(2,1)}) custom-call(bf16[2,56,256]{2,1,0:T(8,128)(2,1)S(1)} %get-tuple-element.6.head, bf16[4096,256]{1,0:T(8,128)(2,1)S(1)} %get-tuple-element.7.proj), custom_call_target="tpu_custom_call" | custom-call | tf_op jit(solution)/shard_map/write_out/pallas_call | solution.py:303
  (3 shorter events, 0.1 us)
Async XLA Ops:
  0.6 1.9 %copy-start = (bf16[1,1,2,56,256]{4,3,2,1,0:T(8,128)(2,1)S(1)}, bf16[1,1,2,56,256]{4,3,2,1,0:T(8,128)(2,1)}, u32[]{:S(2)}) copy-start(bf16[1,1,2,56,256]{4,3,2,1,0:T(8,128)(2,1)} %param.4) | copy-start | bytes 172036
